TPU v7x, 512 devices: a whole 4x8x8 slice. The times are simulated.
512 devices in a mesh: row: 64 (over y, x, core), col: 8 (over z).
Axes of the slice: x: 4, y: 8, z: 8, core: 2. Of those that a mesh axis runs over, the one named last changes fastest.
Arguments:
- hidden_states: bfloat16 [16384, 8192], P('row', 'col'), may hold values from -80 to 80, as said below
- sketch_matrix: bfloat16 [8192, 512], P('col'), may hold values from -0.0625 to 0.0625
Outputs:
- q_left: float32 [16384, 512], P(('row', 'col'))
- q_right: float32 [8, 1024, 512], P('col', 'row')
- triangle: float32 [512, 512], replicated
Inputs may be any that keep to these rules, and one draw needn't show every extreme that they name: `hidden_states`: real-valued activation rows.
All inputs are finite; a program needn't handle non-finite values.
Results may differ from a plain program's by a relative error of at most 0.0023.
Values may be sent and summed in bfloat16 or wider, within the bound.
No kernel may reach another device: no remote copies, remote signals or barrier semaphores. Data moves between devices by JAX's collectives and lax.ppermute only.
A program may use at most 64 MiB of HBM per device.

v0:
```python
import functools
import math

import jax
import jax.numpy as jnp
from jax import lax
from jax.experimental import pallas as pl
from jax.experimental.pallas import tpu as pltpu
from jax.sharding import Mesh
from jax.sharding import PartitionSpec as P

HIGHEST = lax.Precision.HIGHEST
BLOCK = 128
ENOUGH = 0.05
ROW = ("y", "x", "core")


def across_lanes(piece, column):
    place = jnp.full(piece.shape, column, jnp.int32)
    return jnp.take_along_axis(piece, place, axis=1, mode="promise_in_bounds")


def across_rows(piece, row):
    return jnp.broadcast_to(piece[row : row + 1, :], piece.shape)


def eliminate(tiles, finished, group):
    row = lax.broadcasted_iota(jnp.int32, (8, BLOCK), 0)
    lane = lax.broadcasted_iota(jnp.int32, (8, BLOCK), 1) - 8 * group
    here = (lane >= 0) & (lane < 8)
    columns = [across_lanes(tiles[group], 8 * group + t) for t in range(8)]
    pivot = [[across_rows(columns[u], t) for u in range(t + 1)] for t in range(8)]
    head = jnp.where(here, jnp.where(lane == row, 1.0, 0.0), tiles[group])
    rows = [across_rows(head, t) for t in range(8)]
    lower = [[None] * 8 for _ in range(8)]
    inverse = [None] * 8
    for t in range(8):
        inverse[t] = 1.0 / pivot[t][t]
        for i in range(t + 1, 8):
            lower[i][t] = pivot[i][t] * inverse[t]
        for i in range(t + 1, 8):
            for j in range(t + 1, i + 1):
                pivot[i][j] = pivot[i][j] - lower[i][t] * pivot[j][t]
            rows[i] = rows[i] - lower[i][t] * rows[t]
    back = [None] * 8
    for t in reversed(range(8)):
        back[t] = rows[t] * inverse[t]
        for s in reversed(range(t + 1, 8)):
            back[t] = back[t] - lower[s][t] * back[s]
    for i in range(group + 1, len(tiles)):
        tile = jnp.where(here, 0.0, tiles[i])
        for t in reversed(range(8)):
            tile = tile - across_lanes(tiles[i], 8 * group + t) * back[t]
        tiles[i] = tile
    done = jnp.zeros((8, BLOCK), jnp.float32)
    for t in range(8):
        done = jnp.where(row == t, rows[t] * lax.rsqrt(pivot[t][t]), done)
    finished.append(jnp.where(lane < 8, done, 0.0))


def inverse_factors(blocks):
    groups = BLOCK // 8
    states = [([block[8 * i : 8 * i + 8, :] for i in range(groups)], []) for block in blocks]
    for group in range(groups):
        for tiles, finished in states:
            eliminate(tiles, finished, group)
    return [jnp.concatenate(finished, axis=0) for _, finished in states]


def times_transposed(left, right):
    return lax.dot_general(
        left,
        right,
        (((1,), (1,)), ((), ())),
        precision=HIGHEST,
        preferred_element_type=jnp.float32,
    )


def factor_blocks(size, *problems):
    def step(index, carry):
        here = pl.ds(pl.multiple_of(index * BLOCK, BLOCK), BLOCK)
        found = inverse_factors([work[here, here] for work, _, _, _ in problems])
        for (_, _, inverse, _), value in zip(problems, found):
            inverse[...] = value
        for block in range(size // BLOCK):
            first, after = block * BLOCK, (block + 1) * BLOCK

            @pl.when(index == block)
            def _(first=first, after=after):
                for work, factor, inverse, rows in problems:
                    last = min(rows + after, work.shape[0])
                    panel = times_transposed(work[first:last, first:after], inverse[...])
                    factor[first:last, first:after] = panel
                    if after < size:
                        below, right = panel[BLOCK:], panel[BLOCK : size - first]
                        work[after:last, after:] -= times_transposed(below, right)

        return carry

    lax.fori_loop(0, size // BLOCK, step, 0)


def diagonal(square, width):
    row = lax.broadcasted_iota(jnp.int32, (BLOCK, BLOCK), 0)
    column = lax.broadcasted_iota(jnp.int32, (BLOCK, BLOCK), 1)
    blocks = [
        jnp.where(row == column, square[i : i + BLOCK, i : i + BLOCK], 0.0)
        for i in range(0, width, BLOCK)
    ]
    return jnp.concatenate([jnp.sum(block, axis=1, keepdims=True) for block in blocks], axis=0)


def place_rows(grams_ref, work_left, work_right=None):
    for group in range(64):
        y, x, core = group // 8, group // 2 % 4, group % 2
        split = (group // 16 + 1) * BLOCK
        came = grams_ref[core, x, 8 * y : 8 * y + 8, :]
        work_left[8 * group : 8 * group + 8, :split] = came[:, :split]
        if work_right is not None:
            mirrored = 8 * (63 - group)
            work_right[mirrored : mirrored + 8, : came.shape[1] - split] = came[:, split:]


def both_kernel(
    scales,
    grams_ref,
    own_ref,
    raw_ref,
    left_ref,
    right_ref,
    triangle_ref,
    margin_ref,
    work_left,
    factor_left,
    inverse_left,
    work_right,
    factor_right,
    inverse_right,
):
    size, own = own_ref.shape[1], own_ref.shape[0]
    place_rows(grams_ref, work_left, work_right)
    before = [diagonal(work, size) for work in (work_left, work_right)]
    row = lax.broadcasted_iota(jnp.int32, (size, size), 0)
    column = lax.broadcasted_iota(jnp.int32, (size, size), 1)
    work_left[size : size + own, :] = own_ref[...]
    work_left[size + own :, :] = jnp.where(row == column, 1.0, 0.0)
    work_right[size:, :] = raw_ref[...]
    factor_blocks(
        size,
        (work_left, factor_left, inverse_left, size + own),
        (work_right, factor_right, inverse_right, work_right.shape[0]),
    )
    left_ref[...] = factor_left[size : size + own, :] * scales[0]
    right_ref[...] = factor_right[size:, :] * scales[1]

    turned = jnp.where(row <= column, factor_left[size + own :, :] * scales[2], 0.0)
    lower = jnp.where(row >= column, factor_right[:size, :], 0.0)
    half = size // 2
    triangle_ref[:half, :half] = gram_rows(turned[:half, :half], lower[:half, :half])
    triangle_ref[:half, half:] = jnp.zeros((half, size - half), jnp.float32)
    bottom = gram_rows(turned[:, half:], lower)
    keep = (row >= column)[half:]
    triangle_ref[half:, :] = jnp.where(keep, bottom, 0.0)
    top = triangle_ref[:half, :half]
    triangle_ref[:half, :half] = jnp.where((row >= column)[:half, :half], top, 0.0)

    after = [diagonal(factor, size) for factor in (factor_left, factor_right)]
    margin = 1.0
    for a, b in zip(after, before):
        share = a * a / b
        share = jnp.where((share > 0.0) & (share < 2.0), share, -1.0)
        margin = jnp.minimum(margin, jnp.min(share, axis=0, keepdims=True))
    margin_ref[...] = jnp.broadcast_to(margin, margin_ref.shape)


def sort_halves(image, image_ref):
    halves, rows, size = image_ref.shape
    image = image.reshape(rows // 16, halves, 16, size)
    for half in range(halves):
        image_ref[half] = image[:, half].reshape(rows, size)


def raw_kernel(turned_ref, sketch_ref, image_ref):
    sketch = sketch_ref[...]
    high = sketch.astype(jnp.bfloat16)
    low = (sketch - high.astype(jnp.float32)).astype(jnp.bfloat16)
    turned = turned_ref[...]
    image = jnp.dot(turned, high, preferred_element_type=jnp.float32)
    image += jnp.dot(turned, low, preferred_element_type=jnp.float32)
    sort_halves(image, image_ref)


def left_kernel(grams_ref, tall_ref, turned_ref, image_ref, work, factor, inverse):
    size = tall_ref.shape[1]
    place_rows(grams_ref, work)
    work[size:, :] = tall_ref[...]
    factor_blocks(size, (work, factor, inverse, work.shape[0]))
    basis_half = factor[size:, :].astype(jnp.bfloat16)
    image = jnp.dot(turned_ref[...], basis_half, preferred_element_type=jnp.float32)
    sort_halves(image, image_ref)


def right_kernel(scales, gram_ref, tall_ref, solved_ref, lower_ref, work, factor, inverse):
    size = gram_ref.shape[0]
    work[:size, :] = gram_ref[...]
    work[size:, :] = tall_ref[...]
    factor_blocks(size, (work, factor, inverse, work.shape[0]))
    solved_ref[...] = factor[size:, :] * scales[0]
    row = lax.broadcasted_iota(jnp.int32, (size, size), 0)
    column = lax.broadcasted_iota(jnp.int32, (size, size), 1)
    lower_ref[...] = jnp.where(row >= column, factor[:size, :] * scales[1], 0.0)


def share_kernel(col_ref, sketch_ref, near_ref, share_ref):
    size = sketch_ref.shape[1]
    groups = size // 8
    column = lax.broadcasted_iota(jnp.int32, (size, groups), 0)
    group = lax.broadcasted_iota(jnp.int32, (size, groups), 1)
    col = col_ref[0:1, :groups]

    def rows(values, order):
        chosen = jnp.where(column == 8 * order + col, 1.0, 0.0)
        chosen = jnp.dot(
            values, chosen, precision=HIGHEST, preferred_element_type=jnp.float32
        )
        return gram_rows(chosen, values)

    left = rows(sketch_ref[...], group)
    right = rows(near_ref[...], groups - 1 - group)
    for first in range(0, groups, 16):
        split = (first // 16 + 1) * BLOCK
        share_ref[first : first + 16, :split] = left[first : first + 16, :split]
        rest = share_ref.shape[1] - split
        share_ref[first : first + 16, split:] = right[first : first + 16, :rest]


def call(kernel, shapes, operands, extra=()):
    size = operands[1].shape[-1]
    scratch = []
    for rows in extra:
        held = pltpu.VMEM((size + rows, size), jnp.float32)
        scratch += [held, held, pltpu.VMEM((BLOCK, BLOCK), jnp.float32)]
    return pl.pallas_call(
        kernel,
        out_shape=[jax.ShapeDtypeStruct(shape, jnp.float32) for shape in shapes],
        in_specs=[pl.BlockSpec(memory_space=pltpu.VMEM)] * len(operands),
        out_specs=[pl.BlockSpec(memory_space=pltpu.VMEM)] * len(shapes),
        scratch_shapes=scratch,
        compiler_params=pltpu.CompilerParams(vmem_limit_bytes=40 * 2**20),
        cost_estimate=pl.CostEstimate(
            flops=2 * size**3, bytes_accessed=8 * size * size, transcendentals=size
        ),
    )(*operands)


def gather(piece, axes):
    copies = jnp.broadcast_to(piece[None], (lax.axis_size(axes),) + piece.shape)
    return lax.all_to_all(copies, axes, 0, 0, tiled=True)


def pack(values):
    power = jnp.clip(jnp.ceil(jnp.log2(jnp.max(jnp.abs(values)))), -100.0, 100.0)
    scaled = (values * jnp.exp2(14.0 - power)).astype(jnp.float16)
    lanes = jnp.full((*values.shape[:-1], 128), power, jnp.float16)
    return jnp.concatenate([scaled, lanes], axis=-1)


def unpack(message):
    size = message.shape[-1] - 128
    power = message[..., size : size + 1].astype(jnp.float32)
    return message[..., :size].astype(jnp.float32) * jnp.exp2(power - 14.0)


def gram_rows(left, right):
    return lax.dot_general(
        left,
        right,
        (((0,), (0,)), ((), ())),
        precision=HIGHEST,
        preferred_element_type=jnp.float32,
    )


def exchange_halves(partial_image):
    return jnp.sum(lax.all_to_all(partial_image, "core", 0, 0, tiled=True), axis=0)


def gather_gram(piece):
    size = piece.size
    eight = gather(piece, ("y", "col")).reshape(-1, size)
    four = gather(eight, ("x",)).reshape(-1, size)
    return gather(four, ("core",)).reshape(size, size)


def by_basis(grams, sketch, turned, scales):
    size, image_rows = sketch.shape[1], 16
    (partial_image,) = call(
        left_kernel,
        [(2, turned.shape[0] // 2, size)],
        [grams, sketch, turned],
        (sketch.shape[0],),
    )
    parts = exchange_halves(partial_image).astype(jnp.bfloat16).reshape(-1, image_rows, size)
    parts = lax.all_to_all(parts, ("y", "x"), 0, 0, tiled=True)
    image = jnp.sum(parts.astype(jnp.float32), axis=0)

    near = gather(image, ("x", "core")).reshape(-1, size)
    start = (lax.axis_index("core") * 4 + lax.axis_index("x")) * (size // 8)
    chosen = lax.dynamic_slice_in_dim(near, start, size // 8, 1)
    share = gram_rows(chosen, near).reshape(size // 8, 4, size // 4)
    share = lax.all_to_all(share, ("y", "col"), 0, 0, tiled=True)
    gram_right = gather_gram(jnp.sum(share, axis=0))
    q_right, triangle = call(
        functools.partial(right_kernel, scales),
        [(image_rows, size), (size, size)],
        [gram_right, image],
        (image_rows,),
    )
    return (q_right, triangle)


def per_device(hidden_states, sketch_matrix):
    rows, block_width = hidden_states.shape
    size = sketch_matrix.shape[1]
    cols, spread = lax.axis_size("col"), lax.axis_size(ROW)
    own_rows, image_rows = rows // cols, block_width // spread
    root_rows, root_width = math.sqrt(rows * spread), math.sqrt(block_width * cols)
    turned = hidden_states.T

    partial_sketch = jnp.dot(hidden_states, sketch_matrix, preferred_element_type=jnp.float32)
    parts = pack(partial_sketch).reshape(cols, own_rows, size + 128)
    own = jnp.sum(unpack(lax.all_to_all(parts, "col", 0, 0, tiled=True)), axis=0)
    sketch = unpack(gather(pack(own), "col")).reshape(rows, size)
    own = lax.dynamic_slice_in_dim(sketch, lax.axis_index("col") * own_rows, own_rows, 0)

    (partial_raw,) = call(raw_kernel, [(2, block_width // 2, size)], [turned, sketch])
    parts = pack(exchange_halves(partial_raw)).reshape(spread // 2, image_rows, size + 128)
    raw = jnp.sum(unpack(lax.all_to_all(parts, ("y", "x"), 0, 0, tiled=True)), axis=0)

    near = gather(raw, "col").reshape(-1, size)
    wide = size + BLOCK
    col = jnp.full((8, 128), lax.axis_index("col"), jnp.int32)
    (share,) = call(share_kernel, [(spread, wide)], [col, sketch, near])
    share = lax.all_to_all(share.reshape(spread, 1, wide), ROW, 0, 0, tiled=True)
    eight = gather(jnp.sum(share, axis=0), ("y", "col")).reshape(spread, wide)
    grams = gather(gather(eight, ("x",)), ("core",))

    scales = (root_rows, root_width, 1.0 / root_width)
    q_left, q_right, triangle, margin = call(
        functools.partial(both_kernel, scales),
        [(own_rows, size), (image_rows, size), (size, size), (8, 128)],
        [grams, own, raw],
        (own_rows + size, image_rows),
    )
    q_right, triangle = lax.cond(
        margin[0, 0] > ENOUGH,
        lambda: (q_right, triangle),
        lambda: by_basis(grams, sketch, turned, scales[1:]),
    )
    return (q_left, q_right.reshape(1, image_rows, size), triangle)


def solution(mesh):
    fine = Mesh(mesh.devices.reshape(8, 4, 2, 8), ROW + ("col",))
    return jax.shard_map(
        per_device,
        mesh=fine,
        in_specs=(P(ROW, "col"), P("col", None)),
        out_specs=(P(ROW + ("col",), None), P("col", ROW, None), P()),
        check_vma=False,
    )
```

profile of v0, /device:TPU:1, one launch (start us, length us, event | category | flops | bytes accessed | tf_op | source)
XLA Modules:
  0.0 189.5 jit_solution(2545584948582052670)
XLA Ops:
  0.6 0.0 copy-start
  0.6 1.2 copy-done
  1.9 2.1 %abs_reduce_fusion.1 = (f32[]{:T(128)}, f32[256,512]{1,0:T(8,128)S(1)}) fusion(bf16[256,1024]{1,0:T(8,128)(2,1)} %param.4, bf16[1024,512]{1,0:T(8,128)(2,1)S(1)} %copy-done), kind=kOutput, calls=%fused_computation.12 | convolution fusion | flops 268697600 | bytes 2097156 | tf_op jit(solution)/shard_map/dot_general | solution.py:331
  4.0 0.0 copy-start.1
  4.8 0.1 multiply_convert_fusion.1
  4.8 0.1 concatenate.9
  4.9 22.3 %all_to_all.79 = f16[8,32,640]{2,1,0:T(8,128)(2,1)S(1)} all-to-all(f16[8,32,640]{2,1,0:T(8,128)(2,1)S(1)} %bitcast.50), channel_id=1, replica_groups=mesh['y'=8,'x'=4,'core'=2,'col'=8] {'col'}, dimensions={0} | all-to-all | bytes 655360 | tf_op jit(solution)/shard_map/all_to_all | solution.py:333
  27.2 0.1 copy.60
  27.4 0.1 multiply_reduce_fusion.1
  27.5 0.6 abs_reduce_fusion.2
  28.9 0.8 broadcast_in_dim.27
  29.7 3.4 %all-to-all-start.8 = ((f16[8,32,640]{2,1,0:T(8,128)(2,1)}), f16[8,32,640]{2,1,0:T(8,128)(2,1)S(1)}, u32[]{:S(2)}, u32[]{:S(2)}) async-start(f16[8,32,640]{2,1,0:T(8,128)(2,1)} %broadcast_in_dim.27), calls=%async_computation.8 | async-start | bytes 655360 | tf_op jit(solution)/shard_map/all_to_all | solution.py:259
  33.1 0.0 copy-done.1
  33.1 0.2 copy.50
  33.3 9.7 %all-to-all-done.8 = f16[8,32,640]{2,1,0:T(8,128)(2,1)S(1)} async-done(((f16[8,32,640]{2,1,0:T(8,128)(2,1)}), f16[8,32,640]{2,1,0:T(8,128)(2,1)S(1)}, u32[]{:S(2)}, u32[]{:S(2)}) %all-to-all-start.8) | async-done | bytes 327712 | tf_op jit(solution)/shard_map/all_to_all | solution.py:259
  43.0 0.1 copy.61
  43.1 0.1 convert_multiply_fusion
  43.3 0.7 shard_map.49
  44.0 10.2 %all_to_all.80 = f32[2,512,512]{2,1,0:T(8,128)} all-to-all(f32[2,512,512]{2,1,0:T(8,128)S(1)} %shard_map.49), channel_id=1, replica_groups=mesh['y'=8,'x'=4,'core'=2,'col'=8] {'core'}, dimensions={0} | all-to-all | bytes 4194304 | tf_op jit(solution)/shard_map/all_to_all | solution.py:286
  54.2 1.9 reduce_sum.64
  56.1 0.7 abs_reduce_fusion
  57.5 0.1 multiply_convert_fusion
  57.7 0.1 concatenate.11
  57.8 28.2 %all_to_all.81 = f16[32,16,640]{2,1,0:T(8,128)(2,1)S(1)} all-to-all(f16[32,16,640]{2,1,0:T(8,128)(2,1)S(1)} %bitcast.45), channel_id=1, replica_groups=mesh['y'=8,'x'=4,'core'=2,'col'=8] {'y','x'}, dimensions={0} | all-to-all | bytes 1310720 | tf_op jit(solution)/shard_map/all_to_all | solution.py:339
  86.0 0.2 copy.62
  86.3 0.1 copy.52
  86.4 0.2 multiply_reduce_fusion.raw_ref
  86.5 0.7 broadcast_in_dim.28
  87.3 3.4 %all-to-all-start.11 = ((f32[8,16,512]{2,1,0:T(8,128)}), f32[8,16,512]{2,1,0:T(8,128)S(1)}, u32[]{:S(2)}, u32[]{:S(2)}) async-start(f32[8,16,512]{2,1,0:T(8,128)} %broadcast_in_dim.28), calls=%async_computation.11 | async-start | bytes 524288 | tf_op jit(solution)/shard_map/all_to_all | solution.py:259
  90.7 9.3 %all-to-all-done.11 = f32[8,16,512]{2,1,0:T(8,128)S(1)} async-done(((f32[8,16,512]{2,1,0:T(8,128)}), f32[8,16,512]{2,1,0:T(8,128)S(1)}, u32[]{:S(2)}, u32[]{:S(2)}) %all-to-all-start.11) | async-done | bytes 262176 | tf_op jit(solution)/shard_map/all_to_all | solution.py:259
  100.0 2.2 %shard_map.50 = f32[64,640]{1,0:T(8,128)S(1)} custom-call(s32[8,128]{1,0:T(8,128)S(1)} %broadcast_in_dim.26.col_ref, f32[256,512]{1,0:T(8,128)S(1)} %bitcast.40, f32[128,512]{1,0:T(8,128)S(1)} %bitcast.37), custom_call_target="tpu_custom_call" | custom-call | flops 268435456 | bytes 2097152 | tf_op jit(solution)/shard_map/pallas_call | solution.py:244
  102.3 0.2 copy.55
  102.5 20.9 %all_to_all.82 = f32[64,1,640]{2,1,0:T(1,128)S(1)} all-to-all(f32[64,1,640]{2,1,0:T(1,128)S(1)} %copy.55), channel_id=1, replica_groups=mesh['y'=8,'x'=4,'core'=2,'col'=8] {'y','x','core'}, dimensions={0} | all-to-all | bytes 327680 | tf_op jit(solution)/shard_map/all_to_all | solution.py:345
  123.4 0.1 reduce_sum.66
  123.5 0.1 broadcast_in_dim.29
  123.6 15.7 %all_to_all.83 = f32[64,1,640]{2,1,0:T(1,128)S(1)} all-to-all(f32[64,1,640]{2,1,0:T(1,128)S(1)} %broadcast_in_dim.29), channel_id=1, replica_groups=mesh['y'=8,'x'=4,'core'=2,'col'=8] {'y','col'}, dimensions={0} | all-to-all | bytes 327680 | tf_op jit(solution)/shard_map/all_to_all | solution.py:259
  139.3 0.9 broadcast_in_dim.31
  140.2 3.5 %all-to-all-start.14 = ((f32[4,64,640]{2,1,0:T(8,128)}), f32[4,64,640]{2,1,0:T(8,128)S(1)}, u32[]{:S(2)}, u32[]{:S(2)}) async-start(f32[4,64,640]{2,1,0:T(8,128)} %broadcast_in_dim.31), calls=%async_computation.14 | async-start | bytes 1310720 | tf_op jit(solution)/shard_map/all_to_all | solution.py:259
  143.7 8.3 %all-to-all-done.14 = f32[4,64,640]{2,1,0:T(8,128)S(1)} async-done(((f32[4,64,640]{2,1,0:T(8,128)}), f32[4,64,640]{2,1,0:T(8,128)S(1)}, u32[]{:S(2)}, u32[]{:S(2)}) %all-to-all-start.14) | async-done | bytes 655392 | tf_op jit(solution)/shard_map/all_to_all | solution.py:259
  152.0 0.1 broadcast_in_dim.32
  152.1 8.0 %all_to_all.84.grams_ref = f32[2,4,64,640]{3,2,1,0:T(8,128)S(1)} all-to-all(f32[2,4,64,640]{3,2,1,0:T(8,128)S(1)} %broadcast_in_dim.32), channel_id=1, replica_groups=mesh['y'=8,'x'=4,'core'=2,'col'=8] {'core'}, dimensions={0} | all-to-all | bytes 2621440 | tf_op jit(solution)/shard_map/all_to_all | solution.py:259
  160.1 27.6 %shard_map.51 = (f32[32,512]{1,0:T(8,128)}, f32[16,512]{1,0:T(8,128)}, f32[512,512]{1,0:T(8,128)}, f32[8,128]{1,0:T(8,128)S(1)}) custom-call(f32[2,4,64,640]{3,2,1,0:T(8,128)S(1)} %all_to_all.84.grams_ref, f32[32,512]{1,0:T(8,128)S(1)} %constant_dynamic-slice_fusion.own_ref, f32[16,512]{1,0:T(8,128)S(1)} %multiply_reduce_fusion.raw_ref), custom_call_target="tpu_custom_call" | custom-call | flops 268435456 | bytes 2097152 | tf_op jit(solution)/shard_map/pallas_call | solution.py:244
  187.7 0.6 slice.27
  189.0 0.3 conditional.1
  (11 shorter events, 0.1 us)
Async XLA Ops:
  0.6 1.2 copy-start
  4.0 29.1 %copy-start.1 = (bf16[256,1024]{1,0:T(8,128)(2,1)S(1)}, bf16[256,1024]{1,0:T(8,128)(2,1)}, u32[]{:S(2)}) copy-start(bf16[256,1024]{1,0:T(8,128)(2,1)} %param.4) | copy-start | bytes 1572868
  29.7 13.3 %all-to-all-start.8 = ((f16[8,32,640]{2,1,0:T(8,128)(2,1)}), f16[8,32,640]{2,1,0:T(8,128)(2,1)S(1)}, u32[]{:S(2)}, u32[]{:S(2)}) async-start(f16[8,32,640]{2,1,0:T(8,128)(2,1)} %broadcast_in_dim.27), calls=%async_computation.8 | async-start | bytes 655360 | tf_op jit(solution)/shard_map/all_to_all | solution.py:259
  87.3 12.8 %all-to-all-start.11 = ((f32[8,16,512]{2,1,0:T(8,128)}), f32[8,16,512]{2,1,0:T(8,128)S(1)}, u32[]{:S(2)}, u32[]{:S(2)}) async-start(f32[8,16,512]{2,1,0:T(8,128)} %broadcast_in_dim.28), calls=%async_computation.11 | async-start | bytes 524288 | tf_op jit(solution)/shard_map/all_to_all | solution.py:259
  140.2 11.8 %all-to-all-start.14 = ((f32[4,64,640]{2,1,0:T(8,128)}), f32[4,64,640]{2,1,0:T(8,128)S(1)}, u32[]{:S(2)}, u32[]{:S(2)}) async-start(f32[4,64,640]{2,1,0:T(8,128)} %broadcast_in_dim.31), calls=%async_computation.14 | async-start | bytes 1310720 | tf_op jit(solution)/shard_map/all_to_all | solution.py:259
where the time goes:
time: 190 us; the launch traced here: 189 us
  blocking collectives  105 us (55%)
  Pallas kernels  30.6 us (16%)
  waiting for transfers between devices  27.3 us (14%)
  starting transfers between devices  10.3 us (5%)
  local copies, waits for them, and re-layouts  5.57 us (3%)
  between operations  4.01 us (2%)
  other arithmetic  3.95 us (2%)
  matrix products  2.1 us (1%)
    pallas_call x3, Pallas kernels, call(): pl.pallas_call(kernel, out_shape=[jax.ShapeDtypeStruct(shape, jnp.float32...  30.6 us
    all_to_all x1, blocking collectives, per_device(): lax.all_to_all(parts, ('y', 'x'), 0, 0, tiled=True)  28.2 us
    all_to_all x3, waiting for transfers between devices, gather(): return lax.all_to_all(copies, axes, 0, 0, tiled=True)  27.3 us
    all_to_all x2, blocking collectives, gather(): return lax.all_to_all(copies, axes, 0, 0, tiled=True)  23.7 us
    all_to_all x1, blocking collectives, per_device(): lax.all_to_all(parts, 'col', 0, 0, tiled=True)  22.3 us
    all_to_all x1, blocking collectives, per_device(): lax.all_to_all(share.reshape(spread, 1, wide), ROW, 0, 0, tiled=True)  20.9 us
    all_to_all x3, starting transfers between devices, gather(): return lax.all_to_all(copies, axes, 0, 0, tiled=True)  10.3 us
    all_to_all x1, blocking collectives, exchange_halves(): lax.all_to_all(partial_image, 'core', 0, 0, tiled=True)  10.2 us
  transfers between devices with their start and end apart: 3, of which 3 were waited for; matrix products, arithmetic and copies ran while one was open for 0% of the time, Pallas kernels for 0%

commit v1 on v0

--- a/solution.py
+++ b/solution.py
@@ -12,6 +12,7 @@
 HIGHEST = lax.Precision.HIGHEST
 BLOCK = 128
 ENOUGH = 0.05
+LANES = 128
 ROW = ("y", "x", "core")
 
 
@@ -181,14 +182,56 @@
         image_ref[half] = image[:, half].reshape(rows, size)
 
 
-def raw_kernel(turned_ref, sketch_ref, image_ref):
-    sketch = sketch_ref[...]
+def pack(values, packed_ref):
+    peak = jnp.max(jnp.max(jnp.abs(values), axis=0, keepdims=True), axis=1, keepdims=True)
+    power = jnp.clip(jnp.ceil(jnp.log2(peak)), -100.0, 100.0)
+    rows, size = values.shape
+    packed_ref[:, :size] = values * jnp.exp2(14.0 - power)
+    packed_ref[:, size:] = jnp.broadcast_to(power, (rows, LANES))
+
+
+def unpack(packed):
+    size = packed.shape[1] - LANES
+    scale = jnp.exp2(packed[:, size:] - 14.0)
+    return packed[:, :size] * jnp.concatenate([scale] * (size // LANES), axis=1)
+
+
+def unpacked_sum(parts_ref):
+    total = unpack(parts_ref[0])
+    for part in range(1, parts_ref.shape[0]):
+        total += unpack(parts_ref[part])
+    return total
+
+
+def sketch_kernel(hidden_ref, matrix_ref, packed_ref):
+    values = jnp.dot(hidden_ref[...], matrix_ref[...], preferred_element_type=jnp.float32)
+    pack(values, packed_ref)
+
+
+def own_kernel(parts_ref, packed_ref):
+    pack(unpacked_sum(parts_ref), packed_ref)
+
+
+def raw_kernel(turned_ref, parts_ref, image_ref, sketch_ref):
+    sketch = jnp.concatenate([unpack(parts_ref[i]) for i in range(parts_ref.shape[0])], axis=0)
+    sketch_ref[...] = sketch
     high = sketch.astype(jnp.bfloat16)
     low = (sketch - high.astype(jnp.float32)).astype(jnp.bfloat16)
     turned = turned_ref[...]
     image = jnp.dot(turned, high, preferred_element_type=jnp.float32)
     image += jnp.dot(turned, low, preferred_element_type=jnp.float32)
     sort_halves(image, image_ref)
+
+
+def halves_kernel(halves_ref, packed_ref):
+    pack(halves_ref[0] + halves_ref[1], packed_ref)
+
+
+def sum_kernel(parts_ref, sum_ref, copies_ref):
+    total = unpacked_sum(parts_ref)
+    sum_ref[...] = total
+    for copy in range(copies_ref.shape[0]):
+        copies_ref[copy] = total
 
 
 def left_kernel(grams_ref, tall_ref, turned_ref, image_ref, work, factor, inverse):
@@ -236,7 +279,7 @@
 
 
 def call(kernel, shapes, operands, extra=()):
-    size = operands[1].shape[-1]
+    size = operands[1].shape[-1] if extra else 0
     scratch = []
     for rows in extra:
         held = pltpu.VMEM((size + rows, size), jnp.float32)
@@ -249,7 +292,9 @@
         scratch_shapes=scratch,
         compiler_params=pltpu.CompilerParams(vmem_limit_bytes=40 * 2**20),
         cost_estimate=pl.CostEstimate(
-            flops=2 * size**3, bytes_accessed=8 * size * size, transcendentals=size
+            flops=1024 * math.prod(shapes[0]) + 2 * size**3,
+            bytes_accessed=8 * math.prod(shapes[0]),
+            transcendentals=size,
         ),
     )(*operands)
 
@@ -257,19 +302,6 @@
 def gather(piece, axes):
     copies = jnp.broadcast_to(piece[None], (lax.axis_size(axes),) + piece.shape)
     return lax.all_to_all(copies, axes, 0, 0, tiled=True)
-
-
-def pack(values):
-    power = jnp.clip(jnp.ceil(jnp.log2(jnp.max(jnp.abs(values)))), -100.0, 100.0)
-    scaled = (values * jnp.exp2(14.0 - power)).astype(jnp.float16)
-    lanes = jnp.full((*values.shape[:-1], 128), power, jnp.float16)
-    return jnp.concatenate([scaled, lanes], axis=-1)
-
-
-def unpack(message):
-    size = message.shape[-1] - 128
-    power = message[..., size : size + 1].astype(jnp.float32)
-    return message[..., :size].astype(jnp.float32) * jnp.exp2(power - 14.0)
 
 
 def gram_rows(left, right):
@@ -328,17 +360,25 @@
     root_rows, root_width = math.sqrt(rows * spread), math.sqrt(block_width * cols)
     turned = hidden_states.T
 
-    partial_sketch = jnp.dot(hidden_states, sketch_matrix, preferred_element_type=jnp.float32)
-    parts = pack(partial_sketch).reshape(cols, own_rows, size + 128)
-    own = jnp.sum(unpack(lax.all_to_all(parts, "col", 0, 0, tiled=True)), axis=0)
-    sketch = unpack(gather(pack(own), "col")).reshape(rows, size)
+    def halved(packed, axes, groups):
+        packed = packed.astype(jnp.float16).reshape(groups, -1, size + LANES)
+        return lax.all_to_all(packed, axes, 0, 0, tiled=True).astype(jnp.float32)
+
+    packed_shape = (rows, size + LANES)
+    (packed,) = call(sketch_kernel, [packed_shape], [hidden_states, sketch_matrix])
+    parts = halved(packed, "col", cols)
+    (packed,) = call(own_kernel, [(own_rows, size + LANES)], [parts])
+    parts = gather(packed.astype(jnp.float16), "col").astype(jnp.float32)
+
+    half = block_width // 2
+    partial_raw, sketch = call(raw_kernel, [(2, half, size), (rows, size)], [turned, parts])
     own = lax.dynamic_slice_in_dim(sketch, lax.axis_index("col") * own_rows, own_rows, 0)
-
-    (partial_raw,) = call(raw_kernel, [(2, block_width // 2, size)], [turned, sketch])
-    parts = pack(exchange_halves(partial_raw)).reshape(spread // 2, image_rows, size + 128)
-    raw = jnp.sum(unpack(lax.all_to_all(parts, ("y", "x"), 0, 0, tiled=True)), axis=0)
-
-    near = gather(raw, "col").reshape(-1, size)
+    halves = lax.all_to_all(partial_raw, "core", 0, 0, tiled=True)
+    (packed,) = call(halves_kernel, [(half, size + LANES)], [halves])
+    parts = halved(packed, ("y", "x"), spread // 2)
+    raw, near = call(sum_kernel, [(image_rows, size), (cols, image_rows, size)], [parts])
+
+    near = lax.all_to_all(near, "col", 0, 0, tiled=True).reshape(-1, size)
     wide = size + BLOCK
     col = jnp.full((8, 128), lax.axis_index("col"), jnp.int32)
     (share,) = call(share_kernel, [(spread, wide)], [col, sketch, near])

time: 190 us -> 183 us (0.963)
  other arithmetic: 3.95 us -> 0.43 us
  between operations: 4.01 us -> 1.7 us
  matrix products: 2.1 us -> 0 us
    all_to_all x3 -> x2, waiting for transfers between devices: 27.3 us -> 17.9 us  [gather(): return lax.all_to_all(copies, axes, 0, 0, tiled=True)]
    all_to_all x0 -> x1, waiting for transfers between devices: none -> 9.34 us  [per_device(): near = lax.all_to_all(near, 'col', 0, 0, tiled=True).reshape(-1, size)]
    all_to_all x3 -> x2, starting transfers between devices: 10.3 us -> 6.92 us  [gather(): return lax.all_to_all(copies, axes, 0, 0, tiled=True)]
    all_to_all x0 -> x1, starting transfers between devices: none -> 3.41 us  [per_device(): near = lax.all_to_all(near, 'col', 0, 0, tiled=True).reshape(-1, size)]
    reduce_sum x3 -> x0, other arithmetic: 2.19 us -> none  [the longest x1 1.89 us: exchange_halves(): jnp.sum(lax.all_to_all(partial_image, 'core', 0, 0, tiled=True), axis=0)]
    dot_general x1 -> x0, matrix products: 2.1 us -> none  [per_device(): jnp.dot(hidden_states, sketch_matrix, preferred_element_type=jnp.float32)]
    pallas_call x3 -> x7, Pallas kernels: 30.6 us -> 32.4 us  [call(): pl.pallas_call(kernel, out_shape=[jax.ShapeDtypeStruct(shape, jnp.float32...]
where the time goes in v1:
time: 183 us; the launch traced here: 182 us
  blocking collectives  105 us (57%)
  Pallas kernels  32.4 us (18%)
  waiting for transfers between devices  27.3 us (15%)
  starting transfers between devices  10.3 us (6%)
  local copies, waits for them, and re-layouts  5.07 us (3%)
    all_to_all x2, blocking collectives, halved(): return lax.all_to_all(packed, axes, 0, 0, tiled=True).astype(jnp.float32)  50.7 us
    pallas_call x7, Pallas kernels, call(): pl.pallas_call(kernel, out_shape=[jax.ShapeDtypeStruct(shape, jnp.float32...  32.4 us
    all_to_all x2, blocking collectives, gather(): return lax.all_to_all(copies, axes, 0, 0, tiled=True)  23.7 us
    all_to_all x1, blocking collectives, per_device(): lax.all_to_all(share.reshape(spread, 1, wide), ROW, 0, 0, tiled=True)  20.9 us
    all_to_all x2, waiting for transfers between devices, gather(): return lax.all_to_all(copies, axes, 0, 0, tiled=True)  17.9 us
    all_to_all x1, waiting for transfers between devices, per_device(): near = lax.all_to_all(near, 'col', 0, 0, tiled=True).reshape(-1, size)  9.34 us
    all_to_all x1, blocking collectives, per_device(): halves = lax.all_to_all(partial_raw, 'core', 0, 0, tiled=True)  9.32 us
    all_to_all x2, starting transfers between devices, gather(): return lax.all_to_all(copies, axes, 0, 0, tiled=True)  6.92 us
  transfers between devices with their start and end apart: 3, of which 3 were waited for; matrix products, arithmetic and copies ran while one was open for 0% of the time, Pallas kernels for 0%

profile of v1, /device:TPU:1, one launch (start us, length us, event | category | flops | bytes accessed | tf_op | source)
XLA Modules:
  0.0 182.1 jit_solution(14998982880738533544)
XLA Ops:
  0.6 0.0 copy-start
  0.6 1.0 copy-done
  1.7 0.0 copy-start.2
  1.7 1.2 copy-done.2
  2.9 0.6 shard_map.49
  3.5 0.0 copy-start.1
  3.5 22.5 %all_to_all.79 = f16[8,32,640]{2,1,0:T(8,128)(2,1)S(1)} all-to-all(f16[8,32,640]{2,1,0:T(8,128)(2,1)S(1)} %bitcast.37), channel_id=1, replica_groups=mesh['y'=8,'x'=4,'core'=2,'col'=8] {'col'}, dimensions={0} | all-to-all | bytes 655360 | tf_op jit(solution)/shard_map/all_to_all | solution.py:365
  26.1 0.1 shard_map.50
  26.2 0.8 broadcast_in_dim.25
  27.0 3.4 %all-to-all-start.8 = ((f16[8,32,640]{2,1,0:T(8,128)(2,1)}), f16[8,32,640]{2,1,0:T(8,128)(2,1)S(1)}, u32[]{:S(2)}, u32[]{:S(2)}) async-start(f16[8,32,640]{2,1,0:T(8,128)(2,1)} %broadcast_in_dim.25), calls=%async_computation.8 | async-start | bytes 655360 | tf_op jit(solution)/shard_map/all_to_all | solution.py:304
  30.4 0.0 copy-done.1
  30.4 0.2 copy.18
  30.6 9.7 %all-to-all-done.8 = f16[8,32,640]{2,1,0:T(8,128)(2,1)S(1)} async-done(((f16[8,32,640]{2,1,0:T(8,128)(2,1)}), f16[8,32,640]{2,1,0:T(8,128)(2,1)S(1)}, u32[]{:S(2)}, u32[]{:S(2)}) %all-to-all-start.8) | async-done | bytes 327712 | tf_op jit(solution)/shard_map/all_to_all | solution.py:304
  40.3 0.8 shard_map.51
  41.1 9.3 %all_to_all.80.halves_ref = f32[2,512,512]{2,1,0:T(8,128)S(1)} all-to-all(f32[2,512,512]{2,1,0:T(8,128)S(1)} %get-tuple-element.36), channel_id=1, replica_groups=mesh['y'=8,'x'=4,'core'=2,'col'=8] {'core'}, dimensions={0} | all-to-all | bytes 4194304 | tf_op jit(solution)/shard_map/all_to_all | solution.py:376
  50.4 0.3 shard_map.52
  50.7 0.1 convert_element_type.38
  50.8 28.2 %all_to_all.81 = f16[32,16,640]{2,1,0:T(8,128)(2,1)S(1)} all-to-all(f16[32,16,640]{2,1,0:T(8,128)(2,1)S(1)} %bitcast.30), channel_id=1, replica_groups=mesh['y'=8,'x'=4,'core'=2,'col'=8] {'y','x'}, dimensions={0} | all-to-all | bytes 1310720 | tf_op jit(solution)/shard_map/all_to_all | solution.py:365
  79.0 0.1 convert_element_type.39.parts_ref
  79.1 0.8 shard_map.53
  79.9 3.4 %all-to-all-start.11 = ((f32[8,16,512]{2,1,0:T(8,128)}), f32[8,16,512]{2,1,0:T(8,128)S(1)}, u32[]{:S(2)}, u32[]{:S(2)}) async-start(f32[8,16,512]{2,1,0:T(8,128)} %get-tuple-element.37), calls=%async_computation.11 | async-start | bytes 524288 | tf_op jit(solution)/shard_map/all_to_all | solution.py:381
  83.4 9.3 %all-to-all-done.11 = f32[8,16,512]{2,1,0:T(8,128)S(1)} async-done(((f32[8,16,512]{2,1,0:T(8,128)}), f32[8,16,512]{2,1,0:T(8,128)S(1)}, u32[]{:S(2)}, u32[]{:S(2)}) %all-to-all-start.11) | async-done | bytes 262176 | tf_op jit(solution)/shard_map/all_to_all | solution.py:381
  92.7 2.2 %shard_map.54 = f32[64,640]{1,0:T(8,128)S(1)} custom-call(s32[8,128]{1,0:T(8,128)S(1)} %broadcast_in_dim.24.col_ref, f32[256,512]{1,0:T(8,128)S(1)} %get-tuple-element.35.sketch_ref, f32[128,512]{1,0:T(8,128)S(1)} %bitcast.28), custom_call_target="tpu_custom_call" | custom-call | flops 41943040 | bytes 327680 | tf_op jit(solution)/shard_map/pallas_call | solution.py:287
  94.9 0.2 copy.19
  95.1 20.9 %all_to_all.82 = f32[64,1,640]{2,1,0:T(1,128)S(1)} all-to-all(f32[64,1,640]{2,1,0:T(1,128)S(1)} %copy.19), channel_id=1, replica_groups=mesh['y'=8,'x'=4,'core'=2,'col'=8] {'y','x','core'}, dimensions={0} | all-to-all | bytes 327680 | tf_op jit(solution)/shard_map/all_to_all | solution.py:385
  116.1 0.1 reduce_sum.36
  116.2 0.1 broadcast_in_dim.26
  116.3 15.7 %all_to_all.83 = f32[64,1,640]{2,1,0:T(1,128)S(1)} all-to-all(f32[64,1,640]{2,1,0:T(1,128)S(1)} %broadcast_in_dim.26), channel_id=1, replica_groups=mesh['y'=8,'x'=4,'core'=2,'col'=8] {'y','col'}, dimensions={0} | all-to-all | bytes 327680 | tf_op jit(solution)/shard_map/all_to_all | solution.py:304
  132.0 0.9 broadcast_in_dim.28
  132.9 3.5 %all-to-all-start.14 = ((f32[4,64,640]{2,1,0:T(8,128)}), f32[4,64,640]{2,1,0:T(8,128)S(1)}, u32[]{:S(2)}, u32[]{:S(2)}) async-start(f32[4,64,640]{2,1,0:T(8,128)} %broadcast_in_dim.28), calls=%async_computation.14 | async-start | bytes 1310720 | tf_op jit(solution)/shard_map/all_to_all | solution.py:304
  136.4 8.3 %all-to-all-done.14 = f32[4,64,640]{2,1,0:T(8,128)S(1)} async-done(((f32[4,64,640]{2,1,0:T(8,128)}), f32[4,64,640]{2,1,0:T(8,128)S(1)}, u32[]{:S(2)}, u32[]{:S(2)}) %all-to-all-start.14) | async-done | bytes 655392 | tf_op jit(solution)/shard_map/all_to_all | solution.py:304
  144.7 0.1 broadcast_in_dim.29
  144.8 8.0 %all_to_all.84.grams_ref = f32[2,4,64,640]{3,2,1,0:T(8,128)S(1)} all-to-all(f32[2,4,64,640]{3,2,1,0:T(8,128)S(1)} %broadcast_in_dim.29), channel_id=1, replica_groups=mesh['y'=8,'x'=4,'core'=2,'col'=8] {'core'}, dimensions={0} | all-to-all | bytes 2621440 | tf_op jit(solution)/shard_map/all_to_all | solution.py:304
  152.7 27.6 %shard_map.55 = (f32[32,512]{1,0:T(8,128)}, f32[16,512]{1,0:T(8,128)}, f32[512,512]{1,0:T(8,128)}, f32[8,128]{1,0:T(8,128)S(1)}) custom-call(f32[2,4,64,640]{3,2,1,0:T(8,128)S(1)} %all_to_all.84.grams_ref, f32[32,512]{1,0:T(8,128)S(1)} %constant_dynamic-slice_fusion.own_ref, f32[16,512]{1,0:T(8,128)S(1)} %get-tuple-element.38.raw_ref), custom_call_target="tpu_custom_call" | custom-call | flops 285212672 | bytes 131072 | tf_op jit(solution)/shard_map/pallas_call | solution.py:287
  180.4 0.6 slice.3
  181.7 0.3 conditional.1
  (7 shorter events, 0.2 us)
Async XLA Ops:
  0.6 1.0 copy-start
  1.7 1.2 copy-start.2
  3.5 27.0 %copy-start.1 = (bf16[256,1024]{1,0:T(8,128)(2,1)S(1)}, bf16[256,1024]{1,0:T(8,128)(2,1)}, u32[]{:S(2)}) copy-start(bf16[256,1024]{1,0:T(8,128)(2,1)} %hidden_ref.1) | copy-start | bytes 1572868
  27.0 13.3 %all-to-all-start.8 = ((f16[8,32,640]{2,1,0:T(8,128)(2,1)}), f16[8,32,640]{2,1,0:T(8,128)(2,1)S(1)}, u32[]{:S(2)}, u32[]{:S(2)}) async-start(f16[8,32,640]{2,1,0:T(8,128)(2,1)} %broadcast_in_dim.25), calls=%async_computation.8 | async-start | bytes 655360 | tf_op jit(solution)/shard_map/all_to_all | solution.py:304
  79.9 12.8 %all-to-all-start.11 = ((f32[8,16,512]{2,1,0:T(8,128)}), f32[8,16,512]{2,1,0:T(8,128)S(1)}, u32[]{:S(2)}, u32[]{:S(2)}) async-start(f32[8,16,512]{2,1,0:T(8,128)} %get-tuple-element.37), calls=%async_computation.11 | async-start | bytes 524288 | tf_op jit(solution)/shard_map/all_to_all | solution.py:381
  132.9 11.8 %all-to-all-start.14 = ((f32[4,64,640]{2,1,0:T(8,128)}), f32[4,64,640]{2,1,0:T(8,128)S(1)}, u32[]{:S(2)}, u32[]{:S(2)}) async-start(f32[4,64,640]{2,1,0:T(8,128)} %broadcast_in_dim.28), calls=%async_computation.14 | async-start | bytes 1310720 | tf_op jit(solution)/shard_map/all_to_all | solution.py:304

commit v2 on v1

--- a/solution.py
+++ b/solution.py
@@ -13,6 +13,7 @@
 BLOCK = 128
 ENOUGH = 0.05
 LANES = 128
+TILES = 4
 ROW = ("y", "x", "core")
 
 
@@ -172,7 +173,7 @@
         share = a * a / b
         share = jnp.where((share > 0.0) & (share < 2.0), share, -1.0)
         margin = jnp.minimum(margin, jnp.min(share, axis=0, keepdims=True))
-    margin_ref[...] = jnp.broadcast_to(margin, margin_ref.shape)
+    margin_ref[0, 0] = margin[0, 0]
 
 
 def sort_halves(image, image_ref):
@@ -185,15 +186,23 @@
 def pack(values, packed_ref):
     peak = jnp.max(jnp.max(jnp.abs(values), axis=0, keepdims=True), axis=1, keepdims=True)
     power = jnp.clip(jnp.ceil(jnp.log2(peak)), -100.0, 100.0)
-    rows, size = values.shape
-    packed_ref[:, :size] = values * jnp.exp2(14.0 - power)
-    packed_ref[:, size:] = jnp.broadcast_to(power, (rows, LANES))
+    values = values * jnp.exp2(14.0 - power)
+    messages, length, _ = packed_ref.shape
+    tiles = values.shape[1] // LANES
+    rows = (length - 8) // tiles
+    for message in range(messages):
+        part = values[(message * rows) % values.shape[0] :][:rows]
+        for tile in range(tiles):
+            columns = part[:, LANES * tile : LANES * (tile + 1)]
+            packed_ref[message, rows * tile : rows * (tile + 1), :] = columns
+        packed_ref[message, tiles * rows :, :] = jnp.broadcast_to(power, (8, LANES))
 
 
 def unpack(packed):
-    size = packed.shape[1] - LANES
-    scale = jnp.exp2(packed[:, size:] - 14.0)
-    return packed[:, :size] * jnp.concatenate([scale] * (size // LANES), axis=1)
+    length = packed.shape[0] - 8
+    scaled = packed[:length] * jnp.exp2(packed[length : length + 1] - 14.0)
+    rows = length // TILES
+    return jnp.concatenate([scaled[rows * i : rows * (i + 1)] for i in range(TILES)], axis=1)
 
 
 def unpacked_sum(parts_ref):
@@ -203,6 +212,10 @@
     return total
 
 
+def unpacked_rows(parts_ref):
+    return jnp.concatenate([unpack(parts_ref[i]) for i in range(parts_ref.shape[0])], axis=0)
+
+
 def sketch_kernel(hidden_ref, matrix_ref, packed_ref):
     values = jnp.dot(hidden_ref[...], matrix_ref[...], preferred_element_type=jnp.float32)
     pack(values, packed_ref)
@@ -213,7 +226,7 @@
 
 
 def raw_kernel(turned_ref, parts_ref, image_ref, sketch_ref):
-    sketch = jnp.concatenate([unpack(parts_ref[i]) for i in range(parts_ref.shape[0])], axis=0)
+    sketch = unpacked_rows(parts_ref)
     sketch_ref[...] = sketch
     high = sketch.astype(jnp.bfloat16)
     low = (sketch - high.astype(jnp.float32)).astype(jnp.bfloat16)
@@ -225,13 +238,6 @@
 
 def halves_kernel(halves_ref, packed_ref):
     pack(halves_ref[0] + halves_ref[1], packed_ref)
-
-
-def sum_kernel(parts_ref, sum_ref, copies_ref):
-    total = unpacked_sum(parts_ref)
-    sum_ref[...] = total
-    for copy in range(copies_ref.shape[0]):
-        copies_ref[copy] = total
 
 
 def left_kernel(grams_ref, tall_ref, turned_ref, image_ref, work, factor, inverse):
@@ -255,25 +261,29 @@
     lower_ref[...] = jnp.where(row >= column, factor[:size, :] * scales[1], 0.0)
 
 
-def share_kernel(col_ref, sketch_ref, near_ref, share_ref):
-    size = sketch_ref.shape[1]
+def chosen_gram_rows(values, col_ref, mirrored):
+    size = values.shape[1]
     groups = size // 8
     column = lax.broadcasted_iota(jnp.int32, (size, groups), 0)
     group = lax.broadcasted_iota(jnp.int32, (size, groups), 1)
-    col = col_ref[0:1, :groups]
-
-    def rows(values, order):
-        chosen = jnp.where(column == 8 * order + col, 1.0, 0.0)
-        chosen = jnp.dot(
-            values, chosen, precision=HIGHEST, preferred_element_type=jnp.float32
-        )
-        return gram_rows(chosen, values)
-
-    left = rows(sketch_ref[...], group)
-    right = rows(near_ref[...], groups - 1 - group)
-    for first in range(0, groups, 16):
+    if mirrored:
+        group = groups - 1 - group
+    chosen = jnp.where(column == 8 * group + col_ref[0:1, :groups], 1.0, 0.0)
+    chosen = jnp.dot(values, chosen, precision=HIGHEST, preferred_element_type=jnp.float32)
+    return gram_rows(chosen, values)
+
+
+def left_share_kernel(col_ref, sketch_ref, left_ref):
+    left_ref[...] = chosen_gram_rows(sketch_ref[...], col_ref, False)
+
+
+def share_kernel(col_ref, left_ref, parts_ref, share_ref, near_ref):
+    near = unpacked_rows(parts_ref)
+    near_ref[...] = near
+    right = chosen_gram_rows(near, col_ref, True)
+    for first in range(0, share_ref.shape[0], 16):
         split = (first // 16 + 1) * BLOCK
-        share_ref[first : first + 16, :split] = left[first : first + 16, :split]
+        share_ref[first : first + 16, :split] = left_ref[first : first + 16, :split]
         rest = share_ref.shape[1] - split
         share_ref[first : first + 16, split:] = right[first : first + 16, :rest]
 
@@ -288,7 +298,10 @@
         kernel,
         out_shape=[jax.ShapeDtypeStruct(shape, jnp.float32) for shape in shapes],
         in_specs=[pl.BlockSpec(memory_space=pltpu.VMEM)] * len(operands),
-        out_specs=[pl.BlockSpec(memory_space=pltpu.VMEM)] * len(shapes),
+        out_specs=[
+            pl.BlockSpec(memory_space=pltpu.SMEM if shape == (1, 1) else pltpu.VMEM)
+            for shape in shapes
+        ],
         scratch_shapes=scratch,
         compiler_params=pltpu.CompilerParams(vmem_limit_bytes=40 * 2**20),
         cost_estimate=pl.CostEstimate(
@@ -360,28 +373,29 @@
     root_rows, root_width = math.sqrt(rows * spread), math.sqrt(block_width * cols)
     turned = hidden_states.T
 
-    def halved(packed, axes, groups):
-        packed = packed.astype(jnp.float16).reshape(groups, -1, size + LANES)
+    def halved(packed, axes):
+        packed = packed.astype(jnp.float16)
         return lax.all_to_all(packed, axes, 0, 0, tiled=True).astype(jnp.float32)
 
-    packed_shape = (rows, size + LANES)
-    (packed,) = call(sketch_kernel, [packed_shape], [hidden_states, sketch_matrix])
-    parts = halved(packed, "col", cols)
-    (packed,) = call(own_kernel, [(own_rows, size + LANES)], [parts])
-    parts = gather(packed.astype(jnp.float16), "col").astype(jnp.float32)
+    many, few = TILES * own_rows + 8, TILES * image_rows + 8
+    (packed,) = call(sketch_kernel, [(cols, many, LANES)], [hidden_states, sketch_matrix])
+    (packed,) = call(own_kernel, [(cols, many, LANES)], [halved(packed, "col")])
+    parts = halved(packed, "col")
 
     half = block_width // 2
     partial_raw, sketch = call(raw_kernel, [(2, half, size), (rows, size)], [turned, parts])
-    own = lax.dynamic_slice_in_dim(sketch, lax.axis_index("col") * own_rows, own_rows, 0)
+    column = lax.axis_index("col")
+    own = lax.dynamic_slice_in_dim(sketch, column * own_rows, own_rows, 0)
     halves = lax.all_to_all(partial_raw, "core", 0, 0, tiled=True)
-    (packed,) = call(halves_kernel, [(half, size + LANES)], [halves])
-    parts = halved(packed, ("y", "x"), spread // 2)
-    raw, near = call(sum_kernel, [(image_rows, size), (cols, image_rows, size)], [parts])
-
-    near = lax.all_to_all(near, "col", 0, 0, tiled=True).reshape(-1, size)
+    (packed,) = call(halves_kernel, [(spread // 2, few, LANES)], [halves])
+    (packed,) = call(own_kernel, [(cols, few, LANES)], [halved(packed, ("y", "x"))])
+    parts = halved(packed, "col")
+
     wide = size + BLOCK
-    col = jnp.full((8, 128), lax.axis_index("col"), jnp.int32)
-    (share,) = call(share_kernel, [(spread, wide)], [col, sketch, near])
+    col = jnp.full((8, 128), column, jnp.int32)
+    (left,) = call(left_share_kernel, [(spread, size)], [col, sketch])
+    share, near = call(share_kernel, [(spread, wide), (cols * image_rows, size)], [col, left, parts])
+    raw = lax.dynamic_slice_in_dim(near, column * image_rows, image_rows, 0)
     share = lax.all_to_all(share.reshape(spread, 1, wide), ROW, 0, 0, tiled=True)
     eight = gather(jnp.sum(share, axis=0), ("y", "col")).reshape(spread, wide)
     grams = gather(gather(eight, ("x",)), ("core",))
@@ -389,7 +403,7 @@
     scales = (root_rows, root_width, 1.0 / root_width)
     q_left, q_right, triangle, margin = call(
         functools.partial(both_kernel, scales),
-        [(own_rows, size), (image_rows, size), (size, size), (8, 128)],
+        [(own_rows, size), (image_rows, size), (size, size), (1, 1)],
         [grams, own, raw],
         (own_rows + size, image_rows),
     )

time: 183 us -> 175 us (0.956)
  blocking collectives: 105 us -> 101 us
  waiting for transfers between devices: 27.3 us -> 24.3 us
    all_to_all x2 -> x1, waiting for transfers between devices: 17.9 us -> 8.25 us  [gather(): return lax.all_to_all(copies, axes, 0, 0, tiled=True)]
    all_to_all x1 -> x2, waiting for transfers between devices: 9.34 us -> 16.1 us  [halved(): return lax.all_to_all(packed, axes, 0, 0, tiled=True).astype(jnp.float32)]
    all_to_all x2 -> x1, starting transfers between devices: 6.92 us -> 3.48 us  [gather(): return lax.all_to_all(copies, axes, 0, 0, tiled=True)]
    all_to_all x1 -> x2, starting transfers between devices: 3.41 us -> 6.79 us  [halved(): return lax.all_to_all(packed, axes, 0, 0, tiled=True).astype(jnp.float32)]
    all_to_all x2, blocking collectives: 50.7 us -> 48.5 us  [halved(): return lax.all_to_all(packed, axes, 0, 0, tiled=True).astype(jnp.float32)]
    pallas_call x7 -> x8, Pallas kernels: 32.4 us -> 31.6 us  [call(): pl.pallas_call(kernel, out_shape=[jax.ShapeDtypeStruct(shape, jnp.float32...]
  transfers between devices with their start and end apart: 3 -> 3, of which waited for: 3 -> 3; matrix products, arithmetic and copies ran while one was open for 0% -> 0% of each run, Pallas kernels for 0% -> 1%
where the time goes in v2:
time: 175 us
  blocking collectives  101 us (58%)
  Pallas kernels  31.6 us (18%)
  waiting for transfers between devices  24.3 us (14%)
  starting transfers between devices  10.3 us (6%)
  local copies, waits for them, and re-layouts  3.73 us (2%)
  other arithmetic  1.85 us (1%)
    all_to_all x2, blocking collectives, halved(): return lax.all_to_all(packed, axes, 0, 0, tiled=True).astype(jnp.float32)  48.5 us
    pallas_call x8, Pallas kernels, call(): pl.pallas_call(kernel, out_shape=[jax.ShapeDtypeStruct(shape, jnp.float32...  31.6 us
    all_to_all x2, blocking collectives, gather(): return lax.all_to_all(copies, axes, 0, 0, tiled=True)  23.7 us
    all_to_all x1, blocking collectives, per_device(): lax.all_to_all(share.reshape(spread, 1, wide), ROW, 0, 0, tiled=True)  19.8 us
    all_to_all x2, waiting for transfers between devices, halved(): return lax.all_to_all(packed, axes, 0, 0, tiled=True).astype(jnp.float32)  16.1 us
    all_to_all x1, blocking collectives, per_device(): halves = lax.all_to_all(partial_raw, 'core', 0, 0, tiled=True)  8.66 us
    all_to_all x1, waiting for transfers between devices, gather(): return lax.all_to_all(copies, axes, 0, 0, tiled=True)  8.25 us
    all_to_all x2, starting transfers between devices, halved(): return lax.all_to_all(packed, axes, 0, 0, tiled=True).astype(jnp.float32)  6.79 us
  transfers between devices with their start and end apart: 3, of which 3 were waited for; matrix products, arithmetic and copies ran while one was open for 0% of the time, Pallas kernels for 1%

profile of v2, /device:TPU:1, one launch (start us, length us, event | category | flops | bytes accessed | tf_op | source)
XLA Modules:
  0.0 174.5 jit_solution(3119462261597314466)
XLA Ops:
  0.6 0.0 copy-start
  0.6 1.0 copy-done
  1.7 0.0 copy-start.2
  1.7 1.2 copy-done.2
  2.9 0.6 shard_map.49
  3.5 0.0 copy-start.1
  3.5 21.4 %all_to_all.79 = f16[8,136,128]{2,1,0:T(8,128)(2,1)S(1)} all-to-all(f16[8,136,128]{2,1,0:T(8,128)(2,1)S(1)} %convert_element_type.40), channel_id=1, replica_groups=mesh['y'=8,'x'=4,'core'=2,'col'=8] {'col'}, dimensions={0} | all-to-all | bytes 557056 | tf_op jit(solution)/shard_map/all_to_all | solution.py:378
  25.0 0.2 shard_map.50
  25.2 0.7 convert_element_type.42
  25.9 3.4 %all-to-all-start.8 = ((f16[8,136,128]{2,1,0:T(8,128)(2,1)}), f16[8,136,128]{2,1,0:T(8,128)(2,1)S(1)}, u32[]{:S(2)}, u32[]{:S(2)}) async-start(f16[8,136,128]{2,1,0:T(8,128)(2,1)} %convert_element_type.42), calls=%async_computation.8 | async-start | bytes 557056 | tf_op jit(solution)/shard_map/all_to_all | solution.py:378
  29.3 0.0 copy-done.1
  29.4 0.2 copy.18
  29.6 9.3 %all-to-all-done.8 = f16[8,136,128]{2,1,0:T(8,128)(2,1)S(1)} async-done(((f16[8,136,128]{2,1,0:T(8,128)(2,1)}), f16[8,136,128]{2,1,0:T(8,128)(2,1)S(1)}, u32[]{:S(2)}, u32[]{:S(2)}) %all-to-all-start.8) | async-done | bytes 278560 | tf_op jit(solution)/shard_map/all_to_all | solution.py:378
  38.9 0.8 shard_map.51
  39.7 8.7 %all_to_all.80.halves_ref = f32[2,512,512]{2,1,0:T(8,128)S(1)} all-to-all(f32[2,512,512]{2,1,0:T(8,128)S(1)} %get-tuple-element.36), channel_id=1, replica_groups=mesh['y'=8,'x'=4,'core'=2,'col'=8] {'core'}, dimensions={0} | all-to-all | bytes 4194304 | tf_op jit(solution)/shard_map/all_to_all | solution.py:389
  48.3 0.3 shard_map.53
  48.6 0.1 convert_element_type.44
  48.7 27.1 %all_to_all.81 = f16[32,72,128]{2,1,0:T(8,128)(2,1)S(1)} all-to-all(f16[32,72,128]{2,1,0:T(8,128)(2,1)S(1)} %convert_element_type.44), channel_id=1, replica_groups=mesh['y'=8,'x'=4,'core'=2,'col'=8] {'y','x'}, dimensions={0} | all-to-all | bytes 1179648 | tf_op jit(solution)/shard_map/all_to_all | solution.py:378
  75.8 0.1 convert_element_type.45.parts_ref
  75.9 0.2 shard_map.54
  76.1 0.7 convert_element_type.46
  76.8 3.4 %all-to-all-start.11 = ((f16[8,72,128]{2,1,0:T(8,128)(2,1)}), f16[8,72,128]{2,1,0:T(8,128)(2,1)S(1)}, u32[]{:S(2)}, u32[]{:S(2)}) async-start(f16[8,72,128]{2,1,0:T(8,128)(2,1)} %convert_element_type.46), calls=%async_computation.11 | async-start | bytes 294912 | tf_op jit(solution)/shard_map/all_to_all | solution.py:378
  80.2 1.3 shard_map.52.left_ref
  81.5 6.8 %all-to-all-done.11 = f16[8,72,128]{2,1,0:T(8,128)(2,1)S(1)} async-done(((f16[8,72,128]{2,1,0:T(8,128)(2,1)}), f16[8,72,128]{2,1,0:T(8,128)(2,1)S(1)}, u32[]{:S(2)}, u32[]{:S(2)}) %all-to-all-start.11) | async-done | bytes 147488 | tf_op jit(solution)/shard_map/all_to_all | solution.py:378
  88.3 0.7 shard_map.55
  89.0 0.2 copy.19
  89.2 19.8 %all_to_all.82 = f32[64,1,640]{2,1,0:T(1,128)S(1)} all-to-all(f32[64,1,640]{2,1,0:T(1,128)S(1)} %copy.19), channel_id=1, replica_groups=mesh['y'=8,'x'=4,'core'=2,'col'=8] {'y','x','core'}, dimensions={0} | all-to-all | bytes 327680 | tf_op jit(solution)/shard_map/all_to_all | solution.py:399
  109.0 0.1 reduce_sum.36
  109.1 0.1 broadcast_in_dim.23
  109.2 15.7 %all_to_all.83 = f32[64,1,640]{2,1,0:T(1,128)S(1)} all-to-all(f32[64,1,640]{2,1,0:T(1,128)S(1)} %broadcast_in_dim.23), channel_id=1, replica_groups=mesh['y'=8,'x'=4,'core'=2,'col'=8] {'y','col'}, dimensions={0} | all-to-all | bytes 327680 | tf_op jit(solution)/shard_map/all_to_all | solution.py:317
  124.9 0.9 broadcast_in_dim.25
  125.8 3.5 %all-to-all-start.14 = ((f32[4,64,640]{2,1,0:T(8,128)}), f32[4,64,640]{2,1,0:T(8,128)S(1)}, u32[]{:S(2)}, u32[]{:S(2)}) async-start(f32[4,64,640]{2,1,0:T(8,128)} %broadcast_in_dim.25), calls=%async_computation.14 | async-start | bytes 1310720 | tf_op jit(solution)/shard_map/all_to_all | solution.py:317
  129.4 8.3 %all-to-all-done.14 = f32[4,64,640]{2,1,0:T(8,128)S(1)} async-done(((f32[4,64,640]{2,1,0:T(8,128)}), f32[4,64,640]{2,1,0:T(8,128)S(1)}, u32[]{:S(2)}, u32[]{:S(2)}) %all-to-all-start.14) | async-done | bytes 655392 | tf_op jit(solution)/shard_map/all_to_all | solution.py:317
  137.6 0.1 broadcast_in_dim.52
  137.7 8.0 %all_to_all.84.grams_ref = f32[2,4,64,640]{3,2,1,0:T(8,128)S(1)} all-to-all(f32[2,4,64,640]{3,2,1,0:T(8,128)S(1)} %broadcast_in_dim.52), channel_id=1, replica_groups=mesh['y'=8,'x'=4,'core'=2,'col'=8] {'core'}, dimensions={0} | all-to-all | bytes 2621440 | tf_op jit(solution)/shard_map/all_to_all | solution.py:317
  145.7 27.7 %shard_map.56 = (f32[32,512]{1,0:T(8,128)}, f32[16,512]{1,0:T(8,128)}, f32[512,512]{1,0:T(8,128)}, f32[1,1]{1,0:T(1,128)}) custom-call(f32[2,4,64,640]{3,2,1,0:T(8,128)S(1)} %all_to_all.84.grams_ref, f32[32,512]{1,0:T(8,128)S(1)} %constant_dynamic-slice_fusion.1.own_ref, f32[16,512]{1,0:T(8,128)S(1)} %constant_dynamic-slice_fusion.raw_ref), custom_call_target="tpu_custom_call" | custom-call | flops 285212672 | bytes 131072 | tf_op jit(solution)/shard_map/pallas_call | solution.py:297
  174.0 0.3 conditional.1
  (8 shorter events, 0.2 us)
Async XLA Ops:
  0.6 1.0 copy-start
  1.7 1.2 copy-start.2
  3.5 25.8 %copy-start.1 = (bf16[256,1024]{1,0:T(8,128)(2,1)S(1)}, bf16[256,1024]{1,0:T(8,128)(2,1)}, u32[]{:S(2)}) copy-start(bf16[256,1024]{1,0:T(8,128)(2,1)} %hidden_ref.1) | copy-start | bytes 1572868
  25.9 12.9 %all-to-all-start.8 = ((f16[8,136,128]{2,1,0:T(8,128)(2,1)}), f16[8,136,128]{2,1,0:T(8,128)(2,1)S(1)}, u32[]{:S(2)}, u32[]{:S(2)}) async-start(f16[8,136,128]{2,1,0:T(8,128)(2,1)} %convert_element_type.42), calls=%async_computation.8 | async-start | bytes 557056 | tf_op jit(solution)/shard_map/all_to_all | solution.py:378
  76.8 11.5 %all-to-all-start.11 = ((f16[8,72,128]{2,1,0:T(8,128)(2,1)}), f16[8,72,128]{2,1,0:T(8,128)(2,1)S(1)}, u32[]{:S(2)}, u32[]{:S(2)}) async-start(f16[8,72,128]{2,1,0:T(8,128)(2,1)} %convert_element_type.46), calls=%async_computation.11 | async-start | bytes 294912 | tf_op jit(solution)/shard_map/all_to_all | solution.py:378
  125.8 11.8 %all-to-all-start.14 = ((f32[4,64,640]{2,1,0:T(8,128)}), f32[4,64,640]{2,1,0:T(8,128)S(1)}, u32[]{:S(2)}, u32[]{:S(2)}) async-start(f32[4,64,640]{2,1,0:T(8,128)} %broadcast_in_dim.25), calls=%async_computation.14 | async-start | bytes 1310720 | tf_op jit(solution)/shard_map/all_to_all | solution.py:317

commit v3 on v2

--- a/solution.py
+++ b/solution.py
@@ -13,6 +13,7 @@
 BLOCK = 128
 ENOUGH = 0.05
 LANES = 128
+SPAN = 8
 TILES = 4
 ROW = ("y", "x", "core")
 
@@ -49,7 +50,7 @@
         back[t] = rows[t] * inverse[t]
         for s in reversed(range(t + 1, 8)):
             back[t] = back[t] - lower[s][t] * back[s]
-    for i in range(group + 1, len(tiles)):
+    for i in range(group + 1, (group // SPAN + 1) * SPAN):
         tile = jnp.where(here, 0.0, tiles[i])
         for t in reversed(range(8)):
             tile = tile - across_lanes(tiles[i], 8 * group + t) * back[t]
@@ -58,14 +59,29 @@
     for t in range(8):
         done = jnp.where(row == t, rows[t] * lax.rsqrt(pivot[t][t]), done)
     finished.append(jnp.where(lane < 8, done, 0.0))
+    return done
 
 
 def inverse_factors(blocks):
     groups = BLOCK // 8
     states = [([block[8 * i : 8 * i + 8, :] for i in range(groups)], []) for block in blocks]
-    for group in range(groups):
-        for tiles, finished in states:
-            eliminate(tiles, finished, group)
+    lane = lax.broadcasted_iota(jnp.int32, (8, BLOCK), 1)
+    for start in range(0, groups, SPAN):
+        stop = start + SPAN
+        whole = [[] for _ in states]
+        for group in range(start, stop):
+            for (tiles, finished), kept in zip(states, whole):
+                kept.append(eliminate(tiles, finished, group))
+        if stop == groups:
+            break
+        later = lane >= 8 * stop
+        for (tiles, finished), kept in zip(states, whole):
+            kept = [jnp.where(later, k, f) for k, f in zip(kept, finished[start:])]
+            kept = jnp.concatenate(kept, axis=0)
+            change = gram_rows(kept, kept)
+            for i in range(stop, groups):
+                tile = jnp.where((lane >= 8 * start) & ~later, 0.0, tiles[i])
+                tiles[i] = tile - change[8 * i : 8 * i + 8, :]
     return [jnp.concatenate(finished, axis=0) for _, finished in states]
 
 
@@ -216,8 +232,27 @@
     return jnp.concatenate([unpack(parts_ref[i]) for i in range(parts_ref.shape[0])], axis=0)
 
 
-def sketch_kernel(hidden_ref, matrix_ref, packed_ref):
-    values = jnp.dot(hidden_ref[...], matrix_ref[...], preferred_element_type=jnp.float32)
+def sketch_kernel(hidden_any, matrix_any, packed_ref, hidden, matrix, arrived):
+    pieces = arrived.shape[0]
+    width = hidden.shape[1] // pieces
+    copies = []
+    for piece in range(pieces):
+        part = pl.ds(piece * width, width)
+        copies.append(
+            (
+                pltpu.make_async_copy(hidden_any.at[:, part], hidden.at[:, part], arrived.at[piece, 0]),
+                pltpu.make_async_copy(matrix_any.at[part, :], matrix.at[part, :], arrived.at[piece, 1]),
+            )
+        )
+    for pair in copies:
+        for copy in pair:
+            copy.start()
+    values = 0.0
+    for piece, pair in enumerate(copies):
+        for copy in pair:
+            copy.wait()
+        part = slice(piece * width, (piece + 1) * width)
+        values += jnp.dot(hidden[:, part], matrix[part, :], preferred_element_type=jnp.float32)
     pack(values, packed_ref)
 
 
@@ -378,7 +413,18 @@
         return lax.all_to_all(packed, axes, 0, 0, tiled=True).astype(jnp.float32)
 
     many, few = TILES * own_rows + 8, TILES * image_rows + 8
-    (packed,) = call(sketch_kernel, [(cols, many, LANES)], [hidden_states, sketch_matrix])
+    packed = pl.pallas_call(
+        sketch_kernel,
+        out_shape=jax.ShapeDtypeStruct((cols, many, LANES), jnp.float32),
+        in_specs=[pl.BlockSpec(memory_space=pl.ANY)] * 2,
+        out_specs=pl.BlockSpec(memory_space=pltpu.VMEM),
+        scratch_shapes=[
+            pltpu.VMEM(hidden_states.shape, jnp.bfloat16),
+            pltpu.VMEM(sketch_matrix.shape, jnp.bfloat16),
+            pltpu.SemaphoreType.DMA((4, 2)),
+        ],
+        compiler_params=pltpu.CompilerParams(vmem_limit_bytes=40 * 2**20),
+    )(hidden_states, sketch_matrix)
     (packed,) = call(own_kernel, [(cols, many, LANES)], [halved(packed, "col")])
     parts = halved(packed, "col")
 

time: 175 us -> 172 us (0.983)
  Pallas kernels: 31.6 us -> 28.7 us
    pallas_call x8 -> x7, Pallas kernels: 31.6 us -> 27.8 us  [call(): pl.pallas_call(kernel, out_shape=[jax.ShapeDtypeStruct(shape, jnp.float32...]
where the time goes in v3:
time: 172 us
  blocking collectives  101 us (59%)
  Pallas kernels  28.7 us (17%)
  waiting for transfers between devices  24.3 us (14%)
  starting transfers between devices  10.3 us (6%)
  local copies, waits for them, and re-layouts  3.73 us (2%)
  other arithmetic  1.85 us (1%)
  between operations  1.73 us (1%)
    all_to_all x2, blocking collectives, halved(): return lax.all_to_all(packed, axes, 0, 0, tiled=True).astype(jnp.float32)  48.5 us
    pallas_call x7, Pallas kernels, call(): pl.pallas_call(kernel, out_shape=[jax.ShapeDtypeStruct(shape, jnp.float32...  27.8 us
    all_to_all x2, blocking collectives, gather(): return lax.all_to_all(copies, axes, 0, 0, tiled=True)  23.7 us
    all_to_all x1, blocking collectives, per_device(): lax.all_to_all(share.reshape(spread, 1, wide), ROW, 0, 0, tiled=True)  19.8 us
    all_to_all x2, waiting for transfers between devices, halved(): return lax.all_to_all(packed, axes, 0, 0, tiled=True).astype(jnp.float32)  16.1 us
    all_to_all x1, blocking collectives, per_device(): halves = lax.all_to_all(partial_raw, 'core', 0, 0, tiled=True)  8.69 us
    all_to_all x1, waiting for transfers between devices, gather(): return lax.all_to_all(copies, axes, 0, 0, tiled=True)  8.25 us
    all_to_all x2, starting transfers between devices, halved(): return lax.all_to_all(packed, axes, 0, 0, tiled=True).astype(jnp.float32)  6.79 us
  transfers between devices with their start and end apart: 3, of which 3 were waited for; matrix products, arithmetic and copies ran while one was open for 0% of the time, Pallas kernels for 1%

profile of v3, /device:TPU:1, one launch (start us, length us, event | category | flops | bytes accessed | tf_op | source)
XLA Modules:
  0.0 171.6 jit_solution(10836567351764365152)
XLA Ops:
  0.6 0.0 copy-start
  0.6 1.0 copy-done
  1.7 0.0 copy-start.2
  1.7 1.2 copy-done.2
  2.9 0.9 shard_map.49
  3.9 0.0 copy-start.1
  3.9 21.4 %all_to_all.79 = f16[8,136,128]{2,1,0:T(8,128)(2,1)S(1)} all-to-all(f16[8,136,128]{2,1,0:T(8,128)(2,1)S(1)} %convert_element_type.40), channel_id=1, replica_groups=mesh['y'=8,'x'=4,'core'=2,'col'=8] {'col'}, dimensions={0} | all-to-all | bytes 557056 | tf_op jit(solution)/shard_map/all_to_all | solution.py:413
  25.3 0.2 shard_map.50
  25.5 0.7 convert_element_type.42
  26.2 3.4 %all-to-all-start.8 = ((f16[8,136,128]{2,1,0:T(8,128)(2,1)}), f16[8,136,128]{2,1,0:T(8,128)(2,1)S(1)}, u32[]{:S(2)}, u32[]{:S(2)}) async-start(f16[8,136,128]{2,1,0:T(8,128)(2,1)} %convert_element_type.42), calls=%async_computation.8 | async-start | bytes 557056 | tf_op jit(solution)/shard_map/all_to_all | solution.py:413
  29.7 0.0 copy-done.1
  29.7 0.2 copy.18
  29.9 9.3 %all-to-all-done.8 = f16[8,136,128]{2,1,0:T(8,128)(2,1)S(1)} async-done(((f16[8,136,128]{2,1,0:T(8,128)(2,1)}), f16[8,136,128]{2,1,0:T(8,128)(2,1)S(1)}, u32[]{:S(2)}, u32[]{:S(2)}) %all-to-all-start.8) | async-done | bytes 278560 | tf_op jit(solution)/shard_map/all_to_all | solution.py:413
  39.2 0.8 shard_map.51
  40.0 8.7 %all_to_all.80.halves_ref = f32[2,512,512]{2,1,0:T(8,128)S(1)} all-to-all(f32[2,512,512]{2,1,0:T(8,128)S(1)} %get-tuple-element.36), channel_id=1, replica_groups=mesh['y'=8,'x'=4,'core'=2,'col'=8] {'core'}, dimensions={0} | all-to-all | bytes 4194304 | tf_op jit(solution)/shard_map/all_to_all | solution.py:435
  48.7 0.3 shard_map.53
  49.0 0.1 convert_element_type.44
  49.1 27.1 %all_to_all.81 = f16[32,72,128]{2,1,0:T(8,128)(2,1)S(1)} all-to-all(f16[32,72,128]{2,1,0:T(8,128)(2,1)S(1)} %convert_element_type.44), channel_id=1, replica_groups=mesh['y'=8,'x'=4,'core'=2,'col'=8] {'y','x'}, dimensions={0} | all-to-all | bytes 1179648 | tf_op jit(solution)/shard_map/all_to_all | solution.py:413
  76.2 0.1 convert_element_type.45.parts_ref
  76.2 0.2 shard_map.54
  76.4 0.7 convert_element_type.46
  77.1 3.4 %all-to-all-start.11 = ((f16[8,72,128]{2,1,0:T(8,128)(2,1)}), f16[8,72,128]{2,1,0:T(8,128)(2,1)S(1)}, u32[]{:S(2)}, u32[]{:S(2)}) async-start(f16[8,72,128]{2,1,0:T(8,128)(2,1)} %convert_element_type.46), calls=%async_computation.11 | async-start | bytes 294912 | tf_op jit(solution)/shard_map/all_to_all | solution.py:413
  80.5 1.3 shard_map.52.left_ref
  81.9 6.8 %all-to-all-done.11 = f16[8,72,128]{2,1,0:T(8,128)(2,1)S(1)} async-done(((f16[8,72,128]{2,1,0:T(8,128)(2,1)}), f16[8,72,128]{2,1,0:T(8,128)(2,1)S(1)}, u32[]{:S(2)}, u32[]{:S(2)}) %all-to-all-start.11) | async-done | bytes 147488 | tf_op jit(solution)/shard_map/all_to_all | solution.py:413
  88.7 0.7 shard_map.55
  89.3 0.2 copy.19
  89.5 19.8 %all_to_all.82 = f32[64,1,640]{2,1,0:T(1,128)S(1)} all-to-all(f32[64,1,640]{2,1,0:T(1,128)S(1)} %copy.19), channel_id=1, replica_groups=mesh['y'=8,'x'=4,'core'=2,'col'=8] {'y','x','core'}, dimensions={0} | all-to-all | bytes 327680 | tf_op jit(solution)/shard_map/all_to_all | solution.py:445
  109.3 0.1 reduce_sum.36
  109.5 0.1 broadcast_in_dim.23
  109.6 15.7 %all_to_all.83 = f32[64,1,640]{2,1,0:T(1,128)S(1)} all-to-all(f32[64,1,640]{2,1,0:T(1,128)S(1)} %broadcast_in_dim.23), channel_id=1, replica_groups=mesh['y'=8,'x'=4,'core'=2,'col'=8] {'y','col'}, dimensions={0} | all-to-all | bytes 327680 | tf_op jit(solution)/shard_map/all_to_all | solution.py:352
  125.3 0.9 broadcast_in_dim.25
  126.2 3.5 %all-to-all-start.14 = ((f32[4,64,640]{2,1,0:T(8,128)}), f32[4,64,640]{2,1,0:T(8,128)S(1)}, u32[]{:S(2)}, u32[]{:S(2)}) async-start(f32[4,64,640]{2,1,0:T(8,128)} %broadcast_in_dim.25), calls=%async_computation.14 | async-start | bytes 1310720 | tf_op jit(solution)/shard_map/all_to_all | solution.py:352
  129.7 8.3 %all-to-all-done.14 = f32[4,64,640]{2,1,0:T(8,128)S(1)} async-done(((f32[4,64,640]{2,1,0:T(8,128)}), f32[4,64,640]{2,1,0:T(8,128)S(1)}, u32[]{:S(2)}, u32[]{:S(2)}) %all-to-all-start.14) | async-done | bytes 655392 | tf_op jit(solution)/shard_map/all_to_all | solution.py:352
  137.9 0.1 broadcast_in_dim.52
  138.0 8.0 %all_to_all.84.grams_ref = f32[2,4,64,640]{3,2,1,0:T(8,128)S(1)} all-to-all(f32[2,4,64,640]{3,2,1,0:T(8,128)S(1)} %broadcast_in_dim.52), channel_id=1, replica_groups=mesh['y'=8,'x'=4,'core'=2,'col'=8] {'core'}, dimensions={0} | all-to-all | bytes 2621440 | tf_op jit(solution)/shard_map/all_to_all | solution.py:352
  146.0 24.4 %shard_map.56 = (f32[32,512]{1,0:T(8,128)}, f32[16,512]{1,0:T(8,128)}, f32[512,512]{1,0:T(8,128)}, f32[1,1]{1,0:T(1,128)}) custom-call(f32[2,4,64,640]{3,2,1,0:T(8,128)S(1)} %all_to_all.84.grams_ref, f32[32,512]{1,0:T(8,128)S(1)} %constant_dynamic-slice_fusion.1.own_ref, f32[16,512]{1,0:T(8,128)S(1)} %constant_dynamic-slice_fusion.raw_ref), custom_call_target="tpu_custom_call" | custom-call | flops 285212672 | bytes 131072 | tf_op jit(solution)/shard_map/pallas_call | solution.py:332
  171.1 0.3 conditional.1
  (8 shorter events, 0.2 us)
Async XLA Ops:
  0.6 1.0 copy-start
  1.7 1.2 copy-start.2
  3.9 25.8 %copy-start.1 = (bf16[256,1024]{1,0:T(8,128)(2,1)S(1)}, bf16[256,1024]{1,0:T(8,128)(2,1)}, u32[]{:S(2)}) copy-start(bf16[256,1024]{1,0:T(8,128)(2,1)} %hidden_any.1) | copy-start | bytes 1572868
  26.2 12.9 %all-to-all-start.8 = ((f16[8,136,128]{2,1,0:T(8,128)(2,1)}), f16[8,136,128]{2,1,0:T(8,128)(2,1)S(1)}, u32[]{:S(2)}, u32[]{:S(2)}) async-start(f16[8,136,128]{2,1,0:T(8,128)(2,1)} %convert_element_type.42), calls=%async_computation.8 | async-start | bytes 557056 | tf_op jit(solution)/shard_map/all_to_all | solution.py:413
  77.1 11.5 %all-to-all-start.11 = ((f16[8,72,128]{2,1,0:T(8,128)(2,1)}), f16[8,72,128]{2,1,0:T(8,128)(2,1)S(1)}, u32[]{:S(2)}, u32[]{:S(2)}) async-start(f16[8,72,128]{2,1,0:T(8,128)(2,1)} %convert_element_type.46), calls=%async_computation.11 | async-start | bytes 294912 | tf_op jit(solution)/shard_map/all_to_all | solution.py:413
  126.2 11.8 %all-to-all-start.14 = ((f32[4,64,640]{2,1,0:T(8,128)}), f32[4,64,640]{2,1,0:T(8,128)S(1)}, u32[]{:S(2)}, u32[]{:S(2)}) async-start(f32[4,64,640]{2,1,0:T(8,128)} %broadcast_in_dim.25), calls=%async_computation.14 | async-start | bytes 1310720 | tf_op jit(solution)/shard_map/all_to_all | solution.py:352
